TPU v7x, 32 devices: a whole 2x2x4 slice. The times are simulated.
32 devices in a mesh: grp: 2 (over y), mem: 4 (over z), tile: 4 (over x, core).
Axes of the slice: x: 2, y: 2, z: 4, core: 2. Of those that a mesh axis runs over, the one named last changes fastest.
Arguments:
- state: bfloat16 [16, 1024, 256], P(('grp', 'mem'), 'tile'), parts along dimension 0, may hold values from -6 to 6
- op_blocks: bfloat16 [16, 128, 256], replicated, may hold values from -0.1875 to 0.1875
- block_kind: int32 [1024, 4], P(('grp', 'tile')), parts along dimension 0, may hold values from 0 to 15, all different within a row
- block_column: int32 [1024, 4], P(('grp', 'tile')), parts along dimension 0, may hold values from 0 to 255
- obs_value: float32 [8, 16384], P(('grp', 'tile'), 'mem'), parts along dimension 0, may hold values from -8 to 8
- obs_error: float32 [8, 16384], P(('grp', 'tile'), 'mem'), parts along dimension 0, may hold values from 0.5 to 2
- obs_frac: float32 [8, 16384], P(('grp', 'tile'), 'mem'), parts along dimension 0, may hold values from 0 to 1
- obs_count: int32 [8], P(('grp', 'tile')), parts along dimension 0, may hold values from 4096 to 16384, as said below
Outputs:
- gram: float32 [16, 4, 8], P(('grp', 'mem'), 'tile'), parts along dimension 0
- proj: float32 [16, 4], P(('grp', 'mem'), 'tile'), parts along dimension 0
There are 2 independent parts, one for each index of `grp`. A program takes and returns all parts, laid end to end along the dimension named above; an argument that names none is the same for every part. Nothing has to cross between parts.
Inputs may be any that keep to these rules, and one draw needn't show every extreme that they name: `block_kind`: the 4 library entries of one observation block are distinct. `obs_count`: in every draw some tile has all 16384 observations live.
All inputs are finite; a program needn't handle non-finite values.
Results may differ from a plain program's by a relative error of at most 0.0033.
Values may be sent and summed in bfloat16 or wider, within the bound.
A program may use at most 64 MiB of HBM per device.

v0:
```python
import functools

import jax
import jax.numpy as jnp
from jax import lax
from jax.experimental import pallas as pl
from jax.experimental.pallas import tpu as pltpu
from jax.sharding import PartitionSpec as P

MESH = pl.DeviceIdType.MESH
UNROLL_LIMIT = 16
F32 = jnp.float32
BF16 = jnp.bfloat16


def each(start, stop, body):
    if stop - start <= UNROLL_LIMIT:
        for i in range(start, stop):
            body(i)
    else:

        def step(i, carry):
            body(i)
            return carry

        lax.fori_loop(start, stop, step, 0)


def kernel(
    n_mem, n_tile, lib_chunks, block_chunk,
    count_ref, state_hbm, lib_hbm, kind_hbm, column_hbm, value_hbm, error_hbm, frac_hbm,
    gram_ref, proj_ref,
    state_ref, lib_ref, kind_ref, column_ref, value_ref, error_ref, frac_ref,
    prior_ref, regrouped_ref, factor_ref, mean_ref, pert_ref, pert16_ref, weighted_ref,
    piece_ref, landed_ref,
    load_sem, lib_sem, send_sem, recv_sem, piece_send_sem, piece_recv_sem,
):
    mem_dev, value_rows, _ = state_ref.shape
    kind_count, obs_width, _ = lib_ref.shape
    per_block, tile_blocks = kind_ref.shape
    own_blocks = tile_blocks // n_mem
    row_count = own_blocks * obs_width
    members = n_mem * mem_dev
    group = n_mem * n_tile
    mem_id = lax.axis_index("mem")
    tile_id = lax.axis_index("tile")
    me = mem_id * n_tile + tile_id

    def far_first(rank):
        return jnp.where(2 * mem_id < n_mem, n_mem - 1 - rank, rank)

    def to_group(body):
        def row(rank):
            peer_mem = far_first(rank)

            @pl.when(peer_mem != mem_id)
            def _():
                body(peer_mem, tile_id)

            each(1, n_tile, lambda shift: body(peer_mem, lax.rem(tile_id + shift, n_tile)))

        each(0, n_mem, row)

    def to_column(body):
        def one(rank):
            peer_mem = far_first(rank)

            @pl.when(peer_mem != mem_id)
            def _():
                body(peer_mem)

        each(0, n_mem, one)

    barrier = pltpu.get_barrier_semaphore()

    def greet(peer_mem, peer_tile):
        pl.semaphore_signal(
            barrier, inc=1, device_id={"mem": peer_mem, "tile": peer_tile}, device_id_type=MESH
        )

    to_group(greet)

    loads = [
        pltpu.make_async_copy(src, dst, load_sem.at[i])
        for i, (src, dst) in enumerate(
            (
                (kind_hbm, kind_ref), (column_hbm, column_ref), (state_hbm, state_ref),
                (value_hbm, value_ref), (error_hbm, error_ref), (frac_hbm, frac_ref),
            )
        )
    ]
    per_chunk = kind_count // lib_chunks
    lib_loads = [
        pltpu.make_async_copy(
            lib_hbm.at[pl.ds(i * per_chunk, per_chunk)],
            lib_ref.at[pl.ds(i * per_chunk, per_chunk)],
            lib_sem.at[i],
        )
        for i in range(lib_chunks)
    ]
    for copy in loads[:3] + lib_loads + loads[3:]:
        copy.start()

    loads[0].wait()
    loads[1].wait()
    loads[2].wait()

    def priors(first_block, wait_lib):
        kinds = kind_ref[:, pl.ds(first_block, block_chunk)]
        columns = column_ref[:, pl.ds(first_block, block_chunk)]
        entry = lax.broadcasted_iota(jnp.int32, (kind_count, block_chunk), 0)
        chosen = jnp.full((kind_count, block_chunk), -1, jnp.int32)
        for k in range(per_block):
            chosen = jnp.where(kinds[k : k + 1, :] == entry, columns[k : k + 1, :], chosen)
        chosen = jnp.transpose(chosen.astype(F32), (1, 0))
        lane = lax.broadcasted_iota(jnp.int32, (block_chunk, value_rows), 1).astype(F32)
        total = jnp.zeros((mem_dev * block_chunk, obs_width), F32)
        for j in range(kind_count):
            pick = jnp.where(chosen[:, j : j + 1] == lane, 1.0, 0.0).astype(BF16)
            picked = jnp.concatenate(
                [
                    jnp.dot(pick, state_ref[m], preferred_element_type=F32).astype(BF16)
                    for m in range(mem_dev)
                ],
                axis=0,
            )
            if wait_lib and j % per_chunk == 0:
                lib_loads[j // per_chunk].wait()
            total = total + lax.dot_general(
                picked, lib_ref[j], (((1,), (1,)), ((), ())), preferred_element_type=F32
            )
        total = total.astype(BF16).reshape(mem_dev, block_chunk, obs_width)
        prior_ref[:, pl.ds(first_block, block_chunk), :] = total

    if tile_blocks == block_chunk:
        priors(0, True)
    else:
        for copy in lib_loads:
            copy.wait()
        each(0, tile_blocks // block_chunk, lambda i: priors(i * block_chunk, False))

    pl.semaphore_wait(barrier, group - 1)

    def regroup(peer, slot):
        return pltpu.make_async_remote_copy(
            src_ref=prior_ref.at[:, pl.ds(pl.multiple_of(peer * own_blocks, own_blocks), own_blocks), :],
            dst_ref=regrouped_ref.at[slot],
            send_sem=send_sem.at[peer],
            recv_sem=recv_sem.at[slot],
            device_id={"mem": peer},
            device_id_type=MESH,
        )

    to_column(lambda peer: regroup(peer, mem_id).start())
    regrouped_ref[mem_id] = prior_ref[:, pl.ds(pl.multiple_of(mem_id * own_blocks, own_blocks), own_blocks), :]

    for copy in loads[3:]:
        copy.wait()
    target = lax.broadcasted_iota(jnp.int32, (n_tile, row_count), 0).astype(F32) + 0.5
    position = tile_id.astype(F32) + frac_ref[...]
    spread = jnp.abs(position - target)
    distance = jnp.minimum(spread, n_tile - spread) / (n_tile / 4.0)
    error = error_ref[...]
    live = mem_id * row_count + lax.broadcasted_iota(jnp.int32, (1, row_count), 1) < count_ref[0]
    inv_var = jnp.where(live, 1.0 / (error * error), 0.0)
    obs_total = float(n_tile * tile_blocks * obs_width)
    factor_ref[...] = inv_var / (1.0 + distance * distance) / obs_total

    to_column(lambda peer: regroup(peer, peer).wait_recv())

    observed = regrouped_ref[...].astype(F32).reshape(members, own_blocks, obs_width)
    mean = jnp.sum(observed, axis=0) / members
    mean_ref[...] = mean
    pert = (observed - mean[None]).astype(BF16).astype(F32)
    pert_ref[...] = pert.reshape(members * own_blocks, obs_width)

    proj = [jnp.zeros((members, obs_width), F32) for _ in range(n_tile)]
    for b in range(own_blocks):
        lanes = slice(b * obs_width, (b + 1) * obs_width)
        block = pert_ref[pl.ds(b, members, stride=own_blocks), :]
        factor = factor_ref[:, lanes]
        innovation = value_ref[:, lanes] - mean_ref[b : b + 1, :]
        pull = factor * innovation
        pert16_ref[:, lanes] = block.astype(BF16)
        weighted_ref[:, lanes] = jnp.concatenate(
            [block * factor[s : s + 1, :] for s in range(n_tile)], axis=0
        ).astype(BF16)
        for s in range(n_tile):
            proj[s] = proj[s] + block * pull[s : s + 1, :]
    gram = lax.dot_general(
        weighted_ref[...], pert16_ref[...], (((1,), (1,)), ((), ())), preferred_element_type=F32
    )
    for s in range(n_tile):
        sums = jnp.sum(proj[s], axis=1, keepdims=True)
        for i in range(n_mem):
            rows = slice(i * mem_dev, (i + 1) * mem_dev)
            piece_ref[s, i, :, 0:members] = gram[s * members : (s + 1) * members][rows]
            piece_ref[s, i, :, members : members + 1] = sums[rows]

    def share(peer_mem, peer_tile, slot):
        peer = peer_mem * n_tile + peer_tile
        return pltpu.make_async_remote_copy(
            src_ref=piece_ref.at[peer_tile, peer_mem],
            dst_ref=landed_ref.at[slot],
            send_sem=piece_send_sem.at[peer],
            recv_sem=piece_recv_sem.at[slot],
            device_id={"mem": peer_mem, "tile": peer_tile},
            device_id_type=MESH,
        )

    to_group(lambda peer_mem, peer_tile: share(peer_mem, peer_tile, me).start())
    landed_ref[me] = piece_ref[tile_id, mem_id]
    to_column(lambda peer: regroup(peer, mem_id).wait_send())
    to_group(lambda peer_mem, peer_tile: share(peer_mem, peer_tile, peer_mem * n_tile + peer_tile).wait_recv())
    result = jnp.sum(landed_ref[...], axis=0)
    gram_ref[...] = result[:, None, 0:members]
    for m in range(mem_dev):
        proj_ref[0:1, m : m + 1] = result[m : m + 1, members : members + 1]
    to_group(lambda peer_mem, peer_tile: share(peer_mem, peer_tile, me).wait_send())


def on_device(
    state, op_blocks, block_kind, block_column, obs_value, obs_error, obs_frac, obs_count
):
    n_mem = lax.axis_size("mem")
    n_tile = lax.axis_size("tile")
    mem_dev = state.shape[0]
    kind_count, obs_width, _ = op_blocks.shape
    tile_blocks, per_block = block_kind.shape
    own_blocks = tile_blocks // n_mem
    row_count = own_blocks * obs_width
    members = n_mem * mem_dev
    group = n_mem * n_tile
    lib_chunks = 4 if kind_count % 4 == 0 else 1
    block_chunk = 128 if tile_blocks % 128 == 0 else tile_blocks
    piece_width = -(-(members + 1) // 128) * 128
    in_hbm = pl.BlockSpec(memory_space=pltpu.HBM)
    gram, proj = pl.pallas_call(
        functools.partial(kernel, n_mem, n_tile, lib_chunks, block_chunk),
        out_shape=(
            jax.ShapeDtypeStruct((mem_dev, 1, members), F32),
            jax.ShapeDtypeStruct((1, mem_dev), F32),
        ),
        in_specs=[pl.BlockSpec(memory_space=pltpu.SMEM)] + [in_hbm] * 7,
        out_specs=(
            pl.BlockSpec(memory_space=pltpu.VMEM),
            pl.BlockSpec(memory_space=pltpu.VMEM),
        ),
        scratch_shapes=[
            pltpu.VMEM(state.shape, BF16),
            pltpu.VMEM(op_blocks.shape, BF16),
            pltpu.VMEM((per_block, tile_blocks), jnp.int32),
            pltpu.VMEM((per_block, tile_blocks), jnp.int32),
            pltpu.VMEM((1, row_count), F32),
            pltpu.VMEM((1, row_count), F32),
            pltpu.VMEM((1, row_count), F32),
            pltpu.VMEM((mem_dev, tile_blocks, obs_width), BF16),
            pltpu.VMEM((n_mem, mem_dev, own_blocks, obs_width), BF16),
            pltpu.VMEM((n_tile, row_count), F32),
            pltpu.VMEM((own_blocks, obs_width), F32),
            pltpu.VMEM((members * own_blocks, obs_width), F32),
            pltpu.VMEM((members, row_count), BF16),
            pltpu.VMEM((n_tile * members, row_count), BF16),
            pltpu.VMEM((n_tile, n_mem, mem_dev, piece_width), F32),
            pltpu.VMEM((group, mem_dev, piece_width), F32),
            pltpu.SemaphoreType.DMA((6,)),
            pltpu.SemaphoreType.DMA((lib_chunks,)),
            pltpu.SemaphoreType.DMA((n_mem,)),
            pltpu.SemaphoreType.DMA((n_mem,)),
            pltpu.SemaphoreType.DMA((group,)),
            pltpu.SemaphoreType.DMA((group,)),
        ],
        compiler_params=pltpu.CompilerParams(
            collective_id=0, has_side_effects=True, vmem_limit_bytes=40 * 1024 * 1024
        ),
    )(
        obs_count,
        *(
            pltpu.with_memory_space_constraint(array, pltpu.HBM)
            for array in (
                state, op_blocks, jnp.transpose(block_kind), jnp.transpose(block_column),
                obs_value, obs_error, obs_frac,
            )
        ),
    )
    return gram, jnp.transpose(proj)


def solution(mesh):
    return jax.shard_map(
        on_device,
        mesh=mesh,
        in_specs=(
            P(("grp", "mem"), "tile", None),
            P(),
            P(("grp", "tile"), None),
            P(("grp", "tile"), None),
            P(("grp", "tile"), "mem"),
            P(("grp", "tile"), "mem"),
            P(("grp", "tile"), "mem"),
            P(("grp", "tile")),
        ),
        out_specs=(P(("grp", "mem"), "tile", None), P(("grp", "mem"), "tile")),
        check_vma=False,
    )
```

profile of v0, /device:TPU:0, one launch (start us, length us, event | category | flops | bytes accessed | tf_op | source)
XLA Modules:
  0.0 16.8 jit_solution(11473256127822498376)
XLA Ops:
  1.3 14.5 %shard_map.95 = (f32[2,1,8]{2,1,0:T(1,128)S(1)}, f32[1,2]{1,0:T(1,128)S(1)}) custom-call(s32[1]{0:T(128)S(6)} %copy.12.count_ref, bf16[2,256,256]{2,1,0:T(8,128)(2,1)} %state_hbm.1, bf16[16,128,256]{2,1,0:T(8,128)(2,1)} %lib_hbm.1, s32[4,128]{1,0:T(4,128)} %bitcast.4, s32[4,128]{1,0:T(4,128)} %bitcast.5, f32[1,4096]{1,0:T(1,128)} %value_hbm.1, ...), custom_call_target="tpu_custom_call" | custom-call | tf_op jit(solution)/shard_map/pallas_call | solution.py:238
  15.8 0.6 %copy.13 = f32[2,1,8]{2,1,0:T(1,128)} copy(f32[2,1,8]{2,1,0:T(1,128)S(1)} %get-tuple-element.8) | data formatting | bytes 128
  16.3 0.5 %copy.14 = f32[2,1]{0,1:T(1,128)} copy(f32[2,1]{0,1:T(1,128)S(1)} %bitcast.3) | data formatting | bytes 16
where the time goes:
time: 17 us; the launch traced here: 16.8 us
  Pallas kernels  14.5 us (85%)
  between operations  1.29 us (8%)
  local copies, waits for them, and re-layouts  1.07 us (6%)
    pallas_call x1, Pallas kernels, on_device(): pl.pallas_call(functools.partial(kernel, n_mem, n_tile, lib_chunks, block...  14.5 us
    unnamed x2, local copies, waits for them, and re-layouts  1.07 us

commit v1 on v0

v1 whole, which is shorter than its diff:
```python
import functools

import jax
import jax.numpy as jnp
from jax import lax
from jax.experimental import pallas as pl
from jax.experimental.pallas import tpu as pltpu
from jax.sharding import PartitionSpec as P

MESH = pl.DeviceIdType.MESH
UNROLL_LIMIT = 16
F32 = jnp.float32
BF16 = jnp.bfloat16


def each(start, stop, body):
    if stop - start <= UNROLL_LIMIT:
        for i in range(start, stop):
            body(i)
    else:

        def step(i, carry):
            body(i)
            return carry

        lax.fori_loop(start, stop, step, 0)


def kernel(
    n_mem, n_tile, n_host, lib_chunks, block_chunk,
    count_ref, state_hbm, lib_hbm, kind_hbm, column_hbm, value_hbm, error_hbm, frac_hbm,
    gram_ref, proj_ref,
    state_ref, lib_ref, kind_ref, column_ref, own_obs_ref, obs_ref,
    prior_ref, regrouped_ref, factor_ref, mean_ref, pert_ref, pert16_ref, weighted_ref,
    piece_ref, landed_ref,
    load_sem, lib_sem, send_sem, recv_sem, obs_send_sem, obs_recv_sem, piece_send_sem, piece_recv_sem,
):
    mem_dev, value_rows, _ = state_ref.shape
    kind_count, obs_width, _ = lib_ref.shape
    per_block, tile_blocks = kind_ref.shape
    own_blocks = tile_blocks // n_mem
    row_count = own_blocks * obs_width
    members = n_mem * mem_dev
    group = n_mem * n_tile
    mem_id = lax.axis_index("mem")
    tile_id = lax.axis_index("tile")
    me = mem_id * n_tile + tile_id
    per_host = n_mem // n_host
    first_host = (n_mem - n_host) // 2
    host = mem_id - first_host
    is_host = jnp.logical_and(mem_id >= first_host, mem_id < first_host + n_host)
    my_host = first_host + mem_id // per_host
    host_blocks = own_blocks * per_host

    def far_first(rank, first, count):
        return jnp.where(2 * mem_id < n_mem, first + count - 1 - rank, first + rank)

    def to_row(peer_mem, body):
        @pl.when(peer_mem != mem_id)
        def _():
            body(peer_mem, tile_id)

        each(1, n_tile, lambda shift: body(peer_mem, lax.rem(tile_id + shift, n_tile)))

    def to_group(body):
        each(0, n_mem, lambda rank: to_row(far_first(rank, 0, n_mem), body))

    def to_hosts(body):
        each(0, n_host, lambda rank: to_row(far_first(rank, first_host, n_host), body))

    def to_column(first, count, body):
        def one(rank):
            peer_mem = far_first(rank, first, count)

            @pl.when(peer_mem != mem_id)
            def _():
                body(peer_mem)

        each(0, count, one)

    barrier = pltpu.get_barrier_semaphore()

    def greet(peer_mem, peer_tile):
        pl.semaphore_signal(
            barrier, inc=1, device_id={"mem": peer_mem, "tile": peer_tile}, device_id_type=MESH
        )

    def greet_column(peer_mem):
        @pl.when(jnp.logical_or(peer_mem < first_host, peer_mem >= first_host + n_host))
        def _():
            greet(peer_mem, tile_id)

    @pl.when(is_host)
    def _():
        to_column(0, n_mem, greet_column)

    to_hosts(greet)

    loads = [
        pltpu.make_async_copy(src, dst, load_sem.at[i])
        for i, (src, dst) in enumerate(
            (
                (kind_hbm, kind_ref), (column_hbm, column_ref), (state_hbm, state_ref),
                (value_hbm, own_obs_ref.at[0]), (error_hbm, own_obs_ref.at[1]), (frac_hbm, own_obs_ref.at[2]),
            )
        )
    ]
    per_chunk = kind_count // lib_chunks
    lib_loads = [
        pltpu.make_async_copy(
            lib_hbm.at[pl.ds(i * per_chunk, per_chunk)],
            lib_ref.at[pl.ds(i * per_chunk, per_chunk)],
            lib_sem.at[i],
        )
        for i in range(lib_chunks)
    ]
    for copy in loads + lib_loads:
        copy.start()

    for copy in loads:
        copy.wait()

    def obs_to_host(owner):
        return pltpu.make_async_remote_copy(
            src_ref=own_obs_ref,
            dst_ref=obs_ref.at[lax.rem(owner, per_host)],
            send_sem=obs_send_sem.at[0],
            recv_sem=obs_recv_sem.at[lax.rem(owner, per_host)],
            device_id={"mem": my_host},
            device_id_type=MESH,
        )

    @pl.when(jnp.logical_not(is_host))
    def _():
        pl.semaphore_wait(barrier, n_host)

    @pl.when(jnp.logical_and(jnp.logical_not(is_host), my_host != mem_id))
    def _():
        obs_to_host(mem_id).start()

    def priors(first_block, wait_lib):
        kinds = kind_ref[:, pl.ds(first_block, block_chunk)]
        columns = column_ref[:, pl.ds(first_block, block_chunk)]
        entry = lax.broadcasted_iota(jnp.int32, (kind_count, block_chunk), 0)
        chosen = jnp.full((kind_count, block_chunk), -1, jnp.int32)
        for k in range(per_block):
            chosen = jnp.where(kinds[k : k + 1, :] == entry, columns[k : k + 1, :], chosen)
        chosen = jnp.transpose(chosen.astype(F32), (1, 0))
        lane = lax.broadcasted_iota(jnp.int32, (block_chunk, value_rows), 1).astype(F32)
        total = jnp.zeros((mem_dev * block_chunk, obs_width), F32)
        for j in range(kind_count):
            pick = jnp.where(chosen[:, j : j + 1] == lane, 1.0, 0.0).astype(BF16)
            picked = jnp.concatenate(
                [
                    jnp.dot(pick, state_ref[m], preferred_element_type=F32).astype(BF16)
                    for m in range(mem_dev)
                ],
                axis=0,
            )
            if wait_lib and j % per_chunk == 0:
                lib_loads[j // per_chunk].wait()
            total = total + lax.dot_general(
                picked, lib_ref[j], (((1,), (1,)), ((), ())), preferred_element_type=F32
            )
        total = total.astype(BF16).reshape(mem_dev, block_chunk, obs_width)
        prior_ref[:, pl.ds(first_block, block_chunk), :] = total

    if tile_blocks == block_chunk:
        priors(0, True)
    else:
        for copy in lib_loads:
            copy.wait()
        each(0, tile_blocks // block_chunk, lambda i: priors(i * block_chunk, False))

    @pl.when(is_host)
    def _():
        pl.semaphore_wait(barrier, group - 1)

    @pl.when(jnp.logical_and(is_host, my_host != mem_id))
    def _():
        obs_to_host(mem_id).start()

    def host_rows_of(peer_mem):
        return pl.ds(pl.multiple_of((peer_mem - first_host) * host_blocks, host_blocks), host_blocks)

    def regroup(peer, slot):
        return pltpu.make_async_remote_copy(
            src_ref=prior_ref.at[:, host_rows_of(peer), :],
            dst_ref=regrouped_ref.at[slot],
            send_sem=send_sem.at[peer],
            recv_sem=recv_sem.at[slot],
            device_id={"mem": peer},
            device_id_type=MESH,
        )

    def regroup_arriving(slot):
        return pltpu.make_async_remote_copy(
            src_ref=prior_ref.at[:, pl.ds(0, host_blocks), :],
            dst_ref=regrouped_ref.at[slot],
            send_sem=send_sem.at[slot],
            recv_sem=recv_sem.at[slot],
            device_id={"mem": slot},
            device_id_type=MESH,
        )

    to_column(first_host, n_host, lambda peer: regroup(peer, mem_id).start())

    def share(peer_mem, peer_tile, slot):
        return pltpu.make_async_remote_copy(
            src_ref=piece_ref.at[peer_tile, peer_mem],
            dst_ref=landed_ref.at[slot],
            send_sem=piece_send_sem.at[peer_mem * n_tile + peer_tile],
            recv_sem=piece_recv_sem.at[slot],
            device_id={"mem": peer_mem, "tile": peer_tile},
            device_id_type=MESH,
        )

    @pl.when(is_host)
    def _():
        regrouped_ref[mem_id] = prior_ref[:, host_rows_of(mem_id), :]

        target = lax.broadcasted_iota(jnp.int32, (n_tile, row_count), 0).astype(F32) + 0.5
        obs_total = float(n_tile * tile_blocks * obs_width)
        for part in range(per_host):
            owner = host * per_host + part

            @pl.when(owner == mem_id)
            def _():
                obs_ref[part] = own_obs_ref[...]

            @pl.when(owner != mem_id)
            def _():
                obs_to_host(owner).wait_recv()

            spread = jnp.abs(tile_id.astype(F32) + obs_ref[part, 2] - target)
            distance = jnp.minimum(spread, n_tile - spread) / (n_tile / 4.0)
            error = obs_ref[part, 1]
            row = lax.broadcasted_iota(jnp.int32, (1, row_count), 1)
            live = owner * row_count + row < count_ref[0]
            inv_var = jnp.where(live, 1.0 / (error * error), 0.0)
            factor_ref[:, part * row_count : (part + 1) * row_count] = (
                inv_var / (1.0 + distance * distance) / obs_total
            )

        to_column(0, n_mem, lambda peer: regroup_arriving(peer).wait_recv())

        observed = regrouped_ref[...].astype(F32).reshape(members, host_blocks, obs_width)
        mean = jnp.sum(observed, axis=0) / members
        mean_ref[...] = mean
        pert = (observed - mean[None]).astype(BF16).astype(F32)
        pert_ref[...] = pert.reshape(members * host_blocks, obs_width)

        proj = [jnp.zeros((members, obs_width), F32) for _ in range(n_tile)]
        for b in range(host_blocks):
            lanes = slice(b * obs_width, (b + 1) * obs_width)
            part, part_block = divmod(b, own_blocks)
            part_lanes = slice(part_block * obs_width, (part_block + 1) * obs_width)
            block = pert_ref[pl.ds(b, members, stride=host_blocks), :]
            factor = factor_ref[:, lanes]
            innovation = obs_ref[part, 0, :, part_lanes] - mean_ref[b : b + 1, :]
            pull = factor * innovation
            pert16_ref[:, lanes] = block.astype(BF16)
            weighted_ref[:, lanes] = jnp.concatenate(
                [block * factor[s : s + 1, :] for s in range(n_tile)], axis=0
            ).astype(BF16)
            for s in range(n_tile):
                proj[s] = proj[s] + block * pull[s : s + 1, :]
        gram = lax.dot_general(
            weighted_ref[...], pert16_ref[...], (((1,), (1,)), ((), ())), preferred_element_type=F32
        )
        for s in range(n_tile):
            sums = jnp.sum(proj[s], axis=1, keepdims=True)
            for i in range(n_mem):
                rows = slice(i * mem_dev, (i + 1) * mem_dev)
                piece_ref[s, i, :, 0:members] = gram[s * members : (s + 1) * members][rows]
                piece_ref[s, i, :, members : members + 1] = sums[rows]

        slot = host * n_tile + tile_id
        to_group(lambda peer_mem, peer_tile: share(peer_mem, peer_tile, slot).start())
        landed_ref[slot] = piece_ref[tile_id, mem_id]

    to_column(first_host, n_host, lambda peer: regroup(peer, mem_id).wait_send())

    @pl.when(my_host != mem_id)
    def _():
        obs_to_host(mem_id).wait_send()

    to_hosts(
        lambda peer_mem, peer_tile: share(
            peer_mem, peer_tile, (peer_mem - first_host) * n_tile + peer_tile
        ).wait_recv()
    )
    result = jnp.sum(landed_ref[...], axis=0)
    gram_ref[...] = result[:, None, 0:members]
    for m in range(mem_dev):
        proj_ref[0:1, m : m + 1] = result[m : m + 1, members : members + 1]

    @pl.when(is_host)
    def _():
        to_group(lambda peer_mem, peer_tile: share(peer_mem, peer_tile, 0).wait_send())


def on_device(
    state, op_blocks, block_kind, block_column, obs_value, obs_error, obs_frac, obs_count
):
    n_mem = lax.axis_size("mem")
    n_tile = lax.axis_size("tile")
    mem_dev = state.shape[0]
    kind_count, obs_width, _ = op_blocks.shape
    tile_blocks, per_block = block_kind.shape
    own_blocks = tile_blocks // n_mem
    row_count = own_blocks * obs_width
    members = n_mem * mem_dev
    group = n_mem * n_tile
    n_host = n_mem // 2 if n_mem == 4 else n_mem
    per_host = n_mem // n_host
    lib_chunks = 4 if kind_count % 4 == 0 else 1
    block_chunk = 128 if tile_blocks % 128 == 0 else tile_blocks
    piece_width = -(-(members + 1) // 128) * 128
    in_hbm = pl.BlockSpec(memory_space=pltpu.HBM)
    gram, proj = pl.pallas_call(
        functools.partial(kernel, n_mem, n_tile, n_host, lib_chunks, block_chunk),
        out_shape=(
            jax.ShapeDtypeStruct((mem_dev, 1, members), F32),
            jax.ShapeDtypeStruct((1, mem_dev), F32),
        ),
        in_specs=[pl.BlockSpec(memory_space=pltpu.SMEM)] + [in_hbm] * 7,
        out_specs=(
            pl.BlockSpec(memory_space=pltpu.VMEM),
            pl.BlockSpec(memory_space=pltpu.VMEM),
        ),
        scratch_shapes=[
            pltpu.VMEM(state.shape, BF16),
            pltpu.VMEM(op_blocks.shape, BF16),
            pltpu.VMEM((per_block, tile_blocks), jnp.int32),
            pltpu.VMEM((per_block, tile_blocks), jnp.int32),
            pltpu.VMEM((3, 1, row_count), F32),
            pltpu.VMEM((per_host, 3, 1, row_count), F32),
            pltpu.VMEM((mem_dev, tile_blocks, obs_width), BF16),
            pltpu.VMEM((n_mem, mem_dev, own_blocks * per_host, obs_width), BF16),
            pltpu.VMEM((n_tile, row_count * per_host), F32),
            pltpu.VMEM((own_blocks * per_host, obs_width), F32),
            pltpu.VMEM((members * own_blocks * per_host, obs_width), F32),
            pltpu.VMEM((members, row_count * per_host), BF16),
            pltpu.VMEM((n_tile * members, row_count * per_host), BF16),
            pltpu.VMEM((n_tile, n_mem, mem_dev, piece_width), F32),
            pltpu.VMEM((n_host * n_tile, mem_dev, piece_width), F32),
            pltpu.SemaphoreType.DMA((6,)),
            pltpu.SemaphoreType.DMA((lib_chunks,)),
            pltpu.SemaphoreType.DMA((n_mem,)),
            pltpu.SemaphoreType.DMA((n_mem,)),
            pltpu.SemaphoreType.DMA((1,)),
            pltpu.SemaphoreType.DMA((per_host,)),
            pltpu.SemaphoreType.DMA((group,)),
            pltpu.SemaphoreType.DMA((n_host * n_tile,)),
        ],
        compiler_params=pltpu.CompilerParams(
            collective_id=0, has_side_effects=True, vmem_limit_bytes=40 * 1024 * 1024
        ),
    )(
        obs_count,
        *(
            pltpu.with_memory_space_constraint(array, pltpu.HBM)
            for array in (
                state, op_blocks, jnp.transpose(block_kind), jnp.transpose(block_column),
                obs_value, obs_error, obs_frac,
            )
        ),
    )
    return gram, jnp.transpose(proj)


def solution(mesh):
    return jax.shard_map(
        on_device,
        mesh=mesh,
        in_specs=(
            P(("grp", "mem"), "tile", None),
            P(),
            P(("grp", "tile"), None),
            P(("grp", "tile"), None),
            P(("grp", "tile"), "mem"),
            P(("grp", "tile"), "mem"),
            P(("grp", "tile"), "mem"),
            P(("grp", "tile")),
        ),
        out_specs=(P(("grp", "mem"), "tile", None), P(("grp", "mem"), "tile")),
        check_vma=False,
    )
```

time: 17 us -> 17.6 us (1.035)
  Pallas kernels: 14.5 us -> 15.1 us
    pallas_call x1, Pallas kernels: 14.5 us -> 15.1 us  [on_device(): pl.pallas_call(functools.partial(kernel, n_mem, n_tile, n_host, lib_chunk...]
where the time goes in v1:
time: 17.6 us; the launch traced here: 17.5 us
  Pallas kernels  15.1 us (86%)
  between operations  1.29 us (7%)
  local copies, waits for them, and re-layouts  1.07 us (6%)
    pallas_call x1, Pallas kernels, on_device(): pl.pallas_call(functools.partial(kernel, n_mem, n_tile, n_host, lib_chunk...  15.1 us
    unnamed x2, local copies, waits for them, and re-layouts  1.07 us

profile of v1, /device:TPU:0, one launch (start us, length us, event | category | flops | bytes accessed | tf_op | source)
XLA Modules:
  0.0 17.5 jit_solution(6196445698285421159)
XLA Ops:
  1.3 15.1 %shard_map.95 = (f32[2,1,8]{2,1,0:T(1,128)S(1)}, f32[1,2]{1,0:T(1,128)S(1)}) custom-call(s32[1]{0:T(128)S(6)} %copy.12.count_ref, bf16[2,256,256]{2,1,0:T(8,128)(2,1)} %state_hbm.1, bf16[16,128,256]{2,1,0:T(8,128)(2,1)} %lib_hbm.1, s32[4,128]{1,0:T(4,128)} %bitcast.4, s32[4,128]{1,0:T(4,128)} %bitcast.5, f32[1,4096]{1,0:T(1,128)} %value_hbm.1, ...), custom_call_target="tpu_custom_call" | custom-call | tf_op jit(solution)/shard_map/pallas_call | solution.py:321
  16.4 0.6 %copy.13 = f32[2,1,8]{2,1,0:T(1,128)} copy(f32[2,1,8]{2,1,0:T(1,128)S(1)} %get-tuple-element.8) | data formatting | bytes 128
  16.9 0.5 %copy.14 = f32[2,1]{0,1:T(1,128)} copy(f32[2,1]{0,1:T(1,128)S(1)} %bitcast.3) | data formatting | bytes 16
